TPU v7x, 32 devices: a whole 2x2x4 slice. The times are simulated.
32 devices in a mesh: fsdp: 4 (over y, x), seq: 8 (over z, core).
Axes of the slice: x: 2, y: 2, z: 4, core: 2. Of those that a mesh axis runs over, the one named last changes fastest.
Arguments:
- tokens: bfloat16 [4, 1024, 2048], P('fsdp', 'seq'), may hold values from -6 to 6
- gain_one: bfloat16 [2048], P(('fsdp', 'seq')), may hold values from 0.5 to 1.5
- shift_one: bfloat16 [2048], P(('fsdp', 'seq')), may hold values from -3 to 3
- w_qkv: bfloat16 [2048, 3, 2048], P('fsdp', None, 'seq'), may hold values from -0.125 to 0.125
- b_qkv: bfloat16 [3, 2048], P(None, ('fsdp', 'seq')), may hold values from -3 to 3
- w_out: bfloat16 [2048, 2048], P('seq', 'fsdp'), may hold values from -0.5 to 0.5
- gain_two: bfloat16 [2048], P(('fsdp', 'seq')), may hold values from 0.5 to 1.5
- shift_two: bfloat16 [2048], P(('fsdp', 'seq')), may hold values from -3 to 3
- w_gate: bfloat16 [2048, 5632], P('fsdp', 'seq'), may hold values from -0.125 to 0.125
- w_up: bfloat16 [2048, 5632], P('fsdp', 'seq'), may hold values from -0.125 to 0.125
- w_down: bfloat16 [5632, 2048], P('seq', 'fsdp'), may hold values from -0.078125 to 0.078125
- grad_output: bfloat16 [4, 1024, 2048], P('fsdp', 'seq'), may hold values from -6 to 6
Outputs:
- output: bfloat16 [4, 1024, 2048], P('fsdp', 'seq')
- grad_input: float32 [4, 1024, 2048], P('fsdp', 'seq')
- grad_gain_one: float32 [2048], P(('fsdp', 'seq'))
- grad_shift_one: float32 [2048], P(('fsdp', 'seq'))
- grad_w_qkv: float32 [2048, 3, 2048], P('fsdp', None, 'seq')
- grad_b_qkv: float32 [3, 2048], P(None, ('fsdp', 'seq'))
- grad_w_out: float32 [2048, 2048], P('seq', 'fsdp')
- grad_gain_two: float32 [2048], P(('fsdp', 'seq'))
- grad_shift_two: float32 [2048], P(('fsdp', 'seq'))
- grad_w_gate: float32 [2048, 5632], P('fsdp', 'seq')
- grad_w_up: float32 [2048, 5632], P('fsdp', 'seq')
- grad_w_down: float32 [5632, 2048], P('seq', 'fsdp')
All inputs are finite; a program needn't handle non-finite values.
Results may differ from a plain program's by a relative error of at most 0.018.
Values may be sent and summed in bfloat16 or wider, within the bound.
A program may use at most 192 MiB of HBM per device.

v0:
```python
import functools

import jax
import jax.numpy as jnp
import numpy as np
from jax import lax
from jax.experimental import pallas as pl
from jax.experimental.pallas import tpu as pltpu
from jax.sharding import PartitionSpec as P

HEAD = 64
ROT = 16
EPSILON = 1e-05
NEG_LARGE = -1e30
MESH = pl.DeviceIdType.MESH
ANY = pl.BlockSpec(memory_space=pl.ANY)
VMEM = pl.BlockSpec(memory_space=pltpu.VMEM)
BF = jnp.bfloat16
F32 = jnp.float32
VMEM_BYTES = 60 * 2**20
TILE = 512
SMALL = 8


def put(src, dst, send, recv, **device):
    return pltpu.make_async_remote_copy(
        src_ref=src, dst_ref=dst, send_sem=send, recv_sem=recv, device_id=device, device_id_type=MESH
    )


def dot(left, right):
    return jnp.dot(left, right, preferred_element_type=F32)


def dot_nt(left, right):
    return lax.dot_general(left, right, (((1,), (1,)), ((), ())), preferred_element_type=F32)


def dot_tn(left, right):
    return lax.dot_general(left, right, (((0,), (0,)), ((), ())), preferred_element_type=F32)


def aligned(start, size, unit=None):
    return pl.ds(pl.multiple_of(start, unit or size), size)


class Net:
    def __init__(self):
        self.n_f, self.n_s = lax.axis_size("fsdp"), lax.axis_size("seq")
        self.tall = 2 if self.n_f % 2 == 0 else 1
        self.wide = self.n_f // self.tall
        self.n_l = self.n_s // 2
        self.f, self.s = lax.axis_index("fsdp"), lax.axis_index("seq")
        self.a, self.b = self.f // self.wide, self.f % self.wide
        self.z, self.c = self.s // 2, self.s % 2
        self.mate = self.s + 1 - 2 * self.c

    def barrier(self):
        sem = pltpu.get_barrier_semaphore()
        for k in range(1, self.n_f):
            pl.semaphore_signal(
                sem, inc=1, device_id={"fsdp": (self.f + k) % self.n_f}, device_id_type=MESH
            )
        for k in range(1, self.n_s):
            pl.semaphore_signal(
                sem, inc=1, device_id={"seq": (self.s + k) % self.n_s}, device_id_type=MESH
            )
        pl.semaphore_wait(sem, self.n_f + self.n_s - 2)

    def sides(self, hop, act):
        @pl.loop(0, 2)
        def _(side):
            other = self.z + (2 * side - 1) * hop

            @pl.when((other >= 0) & (other < self.n_l))
            def _():
                act(other, side)


class Spread:
    def __init__(self, net, src, part, sems):
        self.net, self.src, self.part, self.sems = net, src, part, sems
        self.rows = [j for j in range(1, net.wide)]
        self.cols = [i for i in range(1, net.tall)]

    @staticmethod
    def count(n_f):
        tall = 2 if n_f % 2 == 0 else 1
        wide = n_f // tall
        return 1 + 2 * (wide - 1) + 2 * (tall - 1) + 4 * (wide - 1) * (tall - 1)

    def at(self, kind, i, j):
        w, t = len(self.rows), len(self.cols)
        base = {
            "own": 0,
            "row": 1,
            "col": 1 + 2 * w,
            "half0": 1 + 2 * w + 2 * t,
            "half1": 1 + 2 * w + 2 * t + 2 * w * t,
        }[kind]
        if kind == "own":
            return self.sems.at[0]
        k = j - 1 if kind == "row" else i - 1 if kind == "col" else (i - 1) * w + j - 1
        return self.sems.at[base + 2 * k], self.sems.at[base + 2 * k + 1]

    def rank(self, i, j):
        net = self.net
        return ((net.a + i) % net.tall) * net.wide + (net.b + j) % net.wide

    def back(self, i, j):
        net = self.net
        return ((net.a - i + net.tall) % net.tall) * net.wide + (net.b - j + net.wide) % net.wide

    def own(self):
        return pltpu.make_async_copy(self.src, self.part(self.net.f, None), self.at("own", 0, 0))

    def first(self, i, j):
        send, recv = self.at("row" if i == 0 else "col", i, j)
        place = self.part(self.net.f, None)
        return put(place, place, send, recv, fsdp=self.rank(i, j))

    def came(self, i, j):
        send, recv = self.at("row" if i == 0 else "col", i, j)
        place = self.part(self.back(i, j), None)
        return put(place, place, send, recv, fsdp=self.rank(i, j))

    def second(self, half, i, j, came=False):
        send, recv = self.at("half0" if half == 0 else "half1", i, j)
        origin = self.back(i, j) if came else self.back(0, j) if half == 0 else self.back(i, 0)
        place = self.part(origin, half)
        return put(place, place, send, recv, fsdp=self.rank(i, 0) if half == 0 else self.rank(0, j))

    def prepare(self):
        self.own().start()

    def start(self):
        self.own().wait()
        for i in self.cols:
            self.first(i, 0).start()
        for j in self.rows:
            self.first(0, j).start()

    def relay(self):
        for j in self.rows:
            self.came(0, j).wait_recv()
            for i in self.cols:
                self.second(0, i, j).start()
        for i in self.cols:
            self.came(i, 0).wait_recv()
            for j in self.rows:
                self.second(1, i, j).start()

    def finish(self):
        for j in self.rows:
            self.first(0, j).wait_send()
        for i in self.cols:
            self.first(i, 0).wait_send()
        for i in self.cols:
            for j in self.rows:
                for half in range(2):
                    self.second(half, i, j, came=True).wait_recv()
                    self.second(half, i, j).wait_send()


class Line:
    def __init__(self, net, src, part, recv, send, local):
        self.net, self.src, self.part, self.recv, self.send, self.local = net, src, part, recv, send, local
        self.pieces = recv.shape[1]
        self.rows = src.shape[0] // self.pieces

    @staticmethod
    def sems(n_s, pieces=2):
        return [
            pltpu.SemaphoreType.DMA((n_s, pieces)),
            pltpu.SemaphoreType.DMA((4, n_s // 2, pieces)),
            pltpu.SemaphoreType.DMA((1,)),
        ]

    def cut(self, ref, piece):
        return ref.at[aligned(piece * self.rows, self.rows)]

    def own(self):
        return pltpu.make_async_copy(self.src, self.part(self.net.s), self.local.at[0])

    def on_line(self, src, chunk, side, hop, piece):
        return put(
            self.cut(src, piece),
            self.cut(self.part(chunk), piece),
            self.send.at[side, hop, piece],
            self.recv.at[chunk, piece],
            seq=self.net.s + 2 - 4 * side,
        )

    def to_mate(self, src, chunk, side, hop, piece):
        return put(
            self.cut(src, piece),
            self.cut(self.part(chunk), piece),
            self.send.at[2 + side, hop, piece],
            self.recv.at[chunk, piece],
            seq=self.net.mate,
        )

    def goes_on(self, side):
        after = self.net.z + 1 - 2 * side
        return (after >= 0) & (after < self.net.n_l)

    def each_piece(self, act):
        pl.loop(0, self.pieces)(act)

    def prepare(self):
        self.own().start()

    def start(self):
        net = self.net
        self.own().wait()
        place = self.part(net.s)

        @self.each_piece
        def _(piece):
            for side in range(2):

                @pl.when(self.goes_on(side))
                def _():
                    self.on_line(place, net.s, side, 0, piece).start()

            self.to_mate(place, net.s, 0, 0, piece).start()

    def came(self, chunk, piece):
        place = self.cut(self.part(chunk), piece)
        put(place, place, self.send.at[0, 0, 0], self.recv.at[chunk, piece], seq=self.net.mate).wait_recv()

    def step(self, hop):
        net = self.net

        @self.each_piece
        def _(piece):
            def act(other, side):
                chunk = 2 * other + net.c
                self.came(chunk, piece)

                @pl.when(self.goes_on(side))
                def _():
                    self.on_line(self.part(chunk), chunk, side, hop, piece).start()

                self.to_mate(self.part(chunk), chunk, side, hop, piece).start()

            net.sides(hop, act)

    def pair(self, other):
        @self.each_piece
        def _(piece):
            self.came(2 * other + 1 - self.net.c, piece)

    def here(self):
        self.pair(self.net.z)

    def finish(self):
        net = self.net
        place = self.part(net.s)

        @self.each_piece
        def _(piece):
            for side in range(2):

                @pl.when(self.goes_on(side))
                def _():
                    self.on_line(place, net.s, side, 0, piece).wait_send()

            self.to_mate(place, net.s, 0, 0, piece).wait_send()

            @pl.loop(1, net.n_l)
            def _(hop):
                def act(other, side):
                    chunk = 2 * other + net.c

                    @pl.when(self.goes_on(side))
                    def _():
                        self.on_line(self.part(chunk), chunk, side, hop, piece).wait_send()

                    self.to_mate(self.part(chunk), chunk, side, hop, piece).wait_send()

                net.sides(hop, act)


class Packets:
    def __init__(self, net, src, buf, sems):
        self.net, self.src, self.buf, self.sems = net, src, buf, sems

    @staticmethod
    def count(n_f, n_s):
        return 1 + 2 * (n_f - 1) + 2 * (n_s - 1)

    def own(self):
        net = self.net
        return pltpu.make_async_copy(self.src, self.buf.at[net.s, net.f], self.sems.at[0])

    def one(self, k, came=False):
        net = self.net
        f = (net.f - k + net.n_f) % net.n_f if came else net.f
        place = self.buf.at[net.s, f]
        return put(
            place if came else self.src,
            place,
            self.sems.at[2 * k - 1],
            self.sems.at[2 * k],
            fsdp=(net.f + k) % net.n_f,
        )

    def two(self, k, came=False):
        net = self.net
        place = self.buf.at[(net.s - k + net.n_s) % net.n_s if came else net.s]
        at = 2 * (net.n_f - 1) + 2 * k - 1
        return put(place, place, self.sems.at[at], self.sems.at[at + 1], seq=(net.s + k) % net.n_s)

    def start(self):
        self.own().start()
        for k in range(1, self.net.n_f):
            self.one(k).start()

    def middle(self):
        self.own().wait()
        for k in range(1, self.net.n_f):
            self.one(k, came=True).wait_recv()
            self.one(k).wait_send()
        for k in range(1, self.net.n_s):
            self.two(k).start()

    def finish(self):
        for k in range(1, self.net.n_s):
            self.two(k, came=True).wait_recv()
            self.two(k).wait_send()

    def unpack(self, out, width):
        net = self.net
        per = 128 // width
        for tile in range(net.n_f * net.n_s // per):
            total = None
            for j in range(per):
                f, s = divmod(tile * per + j, net.n_s)
                piece = self.buf[s, f]
                if j:
                    piece = pltpu.roll(piece, j * width, axis=1)
                total = piece if total is None else total + piece
            out[:, tile * 128 : (tile + 1) * 128] = total


def rotary(values, cosine, sine):
    columns = values.shape[1]
    half = ROT // 2
    times = columns // 128

    def wide(table):
        return table if times == 1 else jnp.concatenate([table] * times, axis=1)

    lane = lax.broadcasted_iota(jnp.int32, values.shape, 1)
    other = jnp.where(
        lane % HEAD < half, pltpu.roll(values, columns - half, axis=1), pltpu.roll(values, half, axis=1)
    )
    return values * wide(cosine) + other * wide(sine)


def rotary_tables(length):
    half = ROT // 2
    freqs = np.float32(10000.0) ** (-np.arange(half, dtype=np.float32) * np.float32(2.0 / ROT))
    angles = np.arange(length, dtype=np.float32)[:, None] * freqs[None, :].astype(np.float32)
    cosine, sine = np.cos(angles), np.sin(angles)
    rest = np.zeros((length, HEAD - ROT), np.float32)
    keep = np.concatenate([cosine, cosine, rest + 1], 1)
    swap = np.concatenate([-sine, sine, rest], 1)
    return [np.tile(t, (1, 128 // HEAD)).astype(np.float32) for t in (keep, swap)]


def normalize(values):
    center = values - jnp.mean(values, -1, keepdims=True)
    inverse = lax.rsqrt(jnp.mean(center * center, -1, keepdims=True) + EPSILON)
    return center * inverse, inverse


class Copies:
    def __init__(self, sems):
        self.sems, self.all, self.open = sems, [], []

    def start(self, src, dst):
        copy = pltpu.make_async_copy(src, dst, self.sems.at[len(self.all)])
        copy.start()
        self.all.append(copy)
        self.open.append(copy)
        return copy

    def wait(self, *copies):
        for copy in copies or list(self.open):
            copy.wait()
            self.open = [c for c in self.open if c is not copy]


def columns_of(ref, depth):
    half_rows = ref.shape[0] // 2

    def part(f, half):
        span = aligned(f * depth, depth)
        if half is None:
            return ref.at[:, span]
        return ref.at[pl.ds(half * half_rows, half_rows), span]

    return part


def rows_of(ref, chunk):
    return lambda s: ref.at[aligned(s * chunk, chunk)]


class Fold:
    def __init__(self, net, tile, total, mate_in, coming, mate_out, out, mate_send, mate_recv, send, recv):
        self.net, self.tile, self.total = net, tile, total
        self.mate_in, self.coming, self.mate_out, self.out = mate_in, coming, mate_out, out
        self.mate_send, self.mate_recv, self.send, self.recv = mate_send, mate_recv, send, recv
        self.chunk = total.shape[0]
        self.pieces = recv.shape[1]
        self.rows = self.chunk // self.pieces

    @staticmethod
    def shared(chunk, width):
        return [pltpu.VMEM((2 * chunk, TILE), F32), pltpu.VMEM((chunk, width), F32)]

    @staticmethod
    def buffers(n_s, chunk, width):
        n_l = n_s // 2
        return [
            pltpu.VMEM((n_l, chunk, width), BF),
            pltpu.VMEM((n_l + 1, chunk, width), BF),
            pltpu.VMEM((3, chunk, width), BF),
            pltpu.VMEM((n_l, chunk, width), BF),
        ]

    @staticmethod
    def sems(n_s, pieces=4):
        n_l = n_s // 2
        return [
            pltpu.SemaphoreType.DMA((3, pieces)),
            pltpu.SemaphoreType.DMA((n_l, pieces)),
            pltpu.SemaphoreType.DMA((n_l, pieces)),
            pltpu.SemaphoreType.DMA((n_l + 1, pieces)),
        ]

    def place(self, other):
        return (other >= 0) & (other < self.net.n_l)

    def fed(self, side):
        return self.place(self.net.z + 1 - 2 * side)

    def span(self, piece):
        return aligned(piece * self.rows, self.rows)

    def each_piece(self, act):
        pl.loop(0, self.pieces)(act)

    def to_mate(self, target, slot, piece):
        span = self.span(piece)
        return put(
            self.mate_out.at[slot, span],
            self.mate_in.at[target, span],
            self.mate_send.at[slot, piece],
            self.mate_recv.at[target, piece],
            seq=self.net.mate,
        )

    def onward(self, target, side, hop, piece):
        span = self.span(piece)
        slot = target + (self.net.n_l - target) * (1 - side) * (1 // hop)
        return put(
            self.out.at[target, span],
            self.coming.at[slot, span],
            self.send.at[target, piece],
            self.recv.at[slot, piece],
            seq=self.net.s + 4 * side - 2,
        )

    def came(self, slot, piece):
        place = self.coming.at[slot, self.span(piece)]
        put(place, place, self.send.at[0, 0], self.recv.at[slot, piece], seq=self.net.mate).wait_recv()

    def mate_sent(self, slot):
        self.each_piece(lambda piece: self.to_mate(self.net.z, slot, piece).wait_send())

    def begin_one(self, target, slot, produce):
        mine = aligned(self.net.c * self.chunk, self.chunk)
        theirs = aligned((1 - self.net.c) * self.chunk, self.chunk)

        def write(cols, value):
            self.tile[...] = value
            self.out[target, :, cols] = self.tile[mine, :].astype(BF)
            self.mate_out[slot, :, cols] = self.tile[theirs, :].astype(BF)

        produce(target, write)
        self.each_piece(lambda piece: self.to_mate(target, slot, piece).start())

    def leave(self, target, side, hop):
        @pl.when((hop > 0) & jnp.logical_not(self.fed(side)))
        def _():
            self.each_piece(lambda piece: self.pass_piece(target, side, hop, piece, False))

    def begin(self, produce, between=None):
        net = self.net

        @pl.loop(0, net.n_l)
        def _(j):
            hop = net.n_l - 1 - j

            def act(target, side):
                @pl.when((hop > 0) | (side == 0))
                def _():
                    @pl.when((hop > 0) & self.place(target + 2 * side - 1))
                    def _():
                        self.mate_sent(side)

                    self.begin_one(target, side + (2 - side) * (1 // (hop + 1)), produce)
                    self.leave(target, side, hop)

            net.sides(hop, act)
            if between is not None:
                pl.when(j == 1)(between)

    def pass_piece(self, target, side, hop, piece, fed):
        self.to_mate(target, 0, piece).wait_recv()
        span = self.span(piece)
        value = self.out[target, span, :].astype(F32) + self.mate_in[target, span, :].astype(F32)
        if fed:
            self.came(target, piece)
            value = value + self.coming[target, span, :].astype(F32)
        self.out[target, span, :] = value.astype(BF)
        self.onward(target, side, hop, piece).start()

    def open_total(self):
        net = self.net

        @self.each_piece
        def _(piece):
            self.to_mate(net.z, 0, piece).wait_recv()
            span = self.span(piece)
            self.total[span, :] = self.out[net.z, span, :].astype(F32) + self.mate_in[net.z, span, :].astype(F32)

    def wave(self, at, near=False, between=None):
        net = self.net
        above = at if near else net.n_l - at

        @pl.loop(0, 2)
        def _(turn):
            side = (1 - (2 * net.z) // net.n_l + turn) % 2
            target = net.n_l - 1 - above + (2 * above - net.n_l + 1) * side
            hop = (target - net.z) * (2 * side - 1)

            @self.each_piece
            def _(piece):
                span = self.span(piece)

                @pl.when(self.fed(side) & (hop > 0))
                def _():
                    self.pass_piece(target, side, hop, piece, True)

                @pl.when(self.fed(side) & (hop == 0))
                def _():
                    slot = net.z + (net.n_l - net.z) * (1 - side)
                    self.came(slot, piece)
                    self.total[span, :] = self.total[span, :] + self.coming[slot, span, :].astype(F32)

                if between is not None:
                    between(((at - 1) * 2 + turn) * self.pieces + piece)

    def finish(self):
        net = self.net
        self.mate_sent(2)
        for side in range(2):
            pl.when(self.place(net.z + 2 * side - 1))(functools.partial(self.mate_sent, side))

        @pl.loop(1, net.n_l)
        def _(hop):
            net.sides(
                hop,
                lambda target, side: self.each_piece(
                    lambda piece: self.onward(target, side, hop, piece).wait_send()
                ),
            )


class GridSum:
    def __init__(self, net, stage, came, sems):
        self.net, self.stage, self.came, self.sems = net, stage, came, sems
        self.half = stage.shape[1] // 2
        self.rows = next(r for r in (176, 128, 96, 64, 32, 16) if self.half % r == 0)
        self.cols = range(1, net.tall)
        self.along = range(1, net.wide)
        self.bases = self.layout(net.n_f)

    @staticmethod
    def layout(n_f):
        tall = 2 if n_f % 2 == 0 else 1
        wide = n_f // tall
        sizes = [(wide - 1) * tall, (tall - 1) * wide, tall - 1, wide - 1]
        return [sum(sizes[:at]) for at in range(5)]

    @staticmethod
    def scratch(n_f, rows, columns):
        count = GridSum.layout(n_f)[4]
        return [
            pltpu.VMEM((n_f, rows, columns), BF),
            pltpu.VMEM((count, rows // 2, columns), BF),
            pltpu.SemaphoreType.DMA((2, count + GridEnd.count(n_f))),
        ]

    def slot(self, kind, i, j):
        base = self.bases[kind]
        return base + [(j - 1) * self.net.tall + i, (i - 1) * self.net.wide + j, i - 1, j - 1][kind]

    def rank(self, i, j):
        net = self.net
        return ((net.a + i) % net.tall) * net.wide + (net.b + j) % net.wide

    def owner(self, at):
        return self.rank(at // self.net.wide, at % self.net.wide)

    def copy(self, kind, i, j):
        half = kind % 2
        along = kind in (0, 3)
        slot = self.slot(kind, i, j)
        at = i * self.net.wide + j
        return put(
            self.stage.at[at, pl.ds(half * self.half, self.half)],
            self.came.at[slot],
            self.sems.at[0, slot],
            self.sems.at[1, slot],
            fsdp=self.rank(0, j) if along else self.rank(i, 0),
        )

    def first(self, at):
        i, j = at // self.net.wide, at % self.net.wide

        @pl.when(j > 0)
        def _():
            self.copy(0, i, j).start()

        @pl.when(i > 0)
        def _():
            self.copy(1, i, j).start()

    def gather(self, half, at, slots, write):
        @pl.loop(0, self.half // self.rows)
        def _(step):
            span = aligned(half * self.half + step * self.rows, self.rows, 16)
            value = self.stage[at, span, :].astype(F32)
            for slot in slots:
                value = value + self.came[slot, aligned(step * self.rows, self.rows, 16), :].astype(F32)
            write(span, value)

    def wait(self, *copies):
        for kind, i, j in copies:
            self.copy(kind, i, j).wait_recv()
        return [self.slot(*copy) for copy in copies]

    def second(self):
        def keep(at):
            def write(span, value):
                self.stage[at, span, :] = value.astype(BF)

            return write

        for i in self.cols:
            at = i * self.net.wide
            self.gather(0, at, self.wait(*[(0, i, j) for j in self.along]), keep(at))
            self.copy(2, i, 0).start()
        for j in self.along:
            self.gather(1, j, self.wait(*[(1, i, j) for i in self.cols]), keep(j))
            self.copy(3, 0, j).start()

    def sum_first(self):
        def keep(at):
            def write(span, value):
                self.stage[at, span, :] = value.astype(BF)

            return write

        for i in range(self.net.tall):
            at = i * self.net.wide
            self.gather(0, at, self.wait(*[(0, i, j) for j in self.along]), keep(at))
        for j in range(self.net.wide):
            self.gather(1, j, self.wait(*[(1, i, j) for i in self.cols]), keep(j))

    def hand_on(self, out):
        net = self.net
        shards = [(0, 0), (0, 1), *[(i * net.wide, 0) for i in self.cols], *[(j, 1) for j in self.along]]
        return [
            pltpu.make_async_copy(
                self.stage.at[at, pl.ds(half * self.half, self.half)], out.at[k], self.sems.at[0, self.bases[4] + k]
            )
            for k, (at, half) in enumerate(shards)
        ]

    def last(self, out):
        def write(span, value):
            out[span, :] = value

        self.gather(
            0, 0, self.wait(*[(0, 0, j) for j in self.along], *[(2, i, 0) for i in self.cols]), write
        )
        self.gather(
            1, 0, self.wait(*[(1, i, 0) for i in self.cols], *[(3, 0, j) for j in self.along]), write
        )

    def finish_first(self):
        for i in range(self.net.tall):
            for j in range(self.net.wide):
                if j:
                    self.copy(0, i, j).wait_send()
                if i:
                    self.copy(1, i, j).wait_send()

    def finish(self):
        self.finish_first()
        for i in self.cols:
            self.copy(2, i, 0).wait_send()
        for j in self.along:
            self.copy(3, 0, j).wait_send()


class GridEnd:
    def __init__(self, net, sums, came, sems):
        self.net, self.sums, self.came, self.sems = net, sums, came, sems

    @staticmethod
    def count(n_f):
        tall = 2 if n_f % 2 == 0 else 1
        return tall + n_f // tall

    @staticmethod
    def scratch(n_f, rows, columns):
        count = GridEnd.count(n_f)
        return [
            pltpu.VMEM((count, rows // 2, columns), BF),
            pltpu.VMEM((count - 2, rows // 2, columns), BF),
            pltpu.SemaphoreType.DMA((2, count - 2)),
        ]

    def copies(self):
        net = self.net
        f = [((net.a + i) % net.tall) * net.wide + net.b for i in range(1, net.tall)]
        f += [net.a * net.wide + (net.b + j) % net.wide for j in range(1, net.wide)]
        return [
            put(self.sums.at[2 + k], self.came.at[k], self.sems.at[0, k], self.sems.at[1, k], fsdp=to)
            for k, to in enumerate(f)
        ]

    def start(self):
        for copy in self.copies():
            copy.start()

    def last(self, out):
        for copy in self.copies():
            copy.wait()
        half = self.sums.shape[1]
        rows = next(r for r in (176, 128, 96, 64, 32, 16) if half % r == 0)
        down = range(self.net.tall - 1)
        along = range(self.net.tall - 1, self.net.tall + self.net.wide - 2)
        for at, slots in enumerate((down, along)):

            @pl.loop(0, half // rows)
            def _(step):
                span = aligned(step * rows, rows, 16)
                value = self.sums[at, span, :].astype(F32)
                for slot in slots:
                    value = value + self.came[slot, span, :].astype(F32)
                out[aligned(at * half + step * rows, rows, 16), :] = value


class PacketSum:
    def __init__(self, net, out, seq_in, total, fsdp_in, sems):
        self.net, self.out, self.seq_in, self.total, self.fsdp_in, self.sems = net, out, seq_in, total, fsdp_in, sems

    @staticmethod
    def scratch(n_f, n_s):
        return [
            pltpu.VMEM((n_s, n_f, SMALL, 128), F32),
            pltpu.VMEM((n_s, n_f, SMALL, 128), F32),
            pltpu.VMEM((n_f, SMALL, 128), F32),
            pltpu.VMEM((n_f, SMALL, 128), F32),
            pltpu.SemaphoreType.DMA((2 * (n_f + n_s),)),
        ]

    def one(self, k):
        to = (self.net.s + k) % self.net.n_s
        return put(self.out.at[to], self.seq_in.at[k], self.sems.at[2 * k], self.sems.at[2 * k + 1], seq=to)

    def two(self, k):
        to = (self.net.f + k) % self.net.n_f
        at = 2 * (self.net.n_s + k)
        return put(self.total.at[to], self.fsdp_in.at[k], self.sems.at[at], self.sems.at[at + 1], fsdp=to)

    def start(self, terms, width):
        net = self.net
        per = 128 // width
        for tile in range(net.n_f * net.n_s // per):
            value = terms[:, tile * 128 : (tile + 1) * 128]
            for j in range(per):
                f, s = divmod(tile * per + j, net.n_s)
                self.out[s, f] = pltpu.roll(value, 128 - j * width, axis=1) if j else value
        for k in range(1, net.n_s):
            self.one(k).start()

    def middle(self):
        net = self.net
        total = self.out[net.s]
        for k in range(1, net.n_s):
            self.one(k).wait()
            total = total + self.seq_in[k]
        self.total[...] = total
        for k in range(1, net.n_f):
            self.two(k).start()

    def finish(self, result):
        net = self.net
        total = self.total[net.f]
        for k in range(1, net.n_f):
            self.two(k).wait()
            total = total + self.fsdp_in[k]
        result[...] = total


def norm_backward(rows, source, grad, gain, terms, at, write):
    terms[at : at + 2, :] = jnp.zeros((2, terms.shape[1]), F32)

    @pl.loop(0, rows // 32)
    def _(i):
        span = aligned(i * 32, 32)
        scaled, inverse = normalize(source[span, :].astype(F32))
        value = grad[span, :]
        upstream = value * gain
        inner = jnp.mean(upstream, -1, keepdims=True)
        cross = jnp.mean(upstream * scaled, -1, keepdims=True)
        terms[at : at + 1, :] = terms[at : at + 1, :] + jnp.sum(value * scaled, 0, keepdims=True)
        terms[at + 1 : at + 2, :] = terms[at + 1 : at + 2, :] + jnp.sum(value, 0, keepdims=True)
        write(i, span, inverse * (upstream - inner - scaled * cross))


def layer_kernel(
    tok,
    gain_one,
    shift_one,
    gain_two,
    shift_two,
    bias,
    wq_own,
    wo_own,
    wg_own,
    wu_own,
    wd_own,
    gout_own,
    cosine,
    sine,
    q_o,
    k_o,
    kt_o,
    v_o,
    att_o,
    lse_o,
    n1_o,
    gains_o,
    wq_o,
    wo_o,
    dm_o,
    datt_o,
    dmid_o,
    top_o,
    terms_o,
    gate_o,
    up_o,
    down_o,
    rows,
    gout,
    wq,
    wo,
    wg,
    wu,
    wd,
    q,
    k,
    kt,
    v,
    vt,
    ot,
    att,
    hidden,
    dgate,
    dup,
    mid,
    low,
    packet,
    packets,
    tiles,
    total,
    *rest,
):
    net = Net()
    chunk, width = tok.shape
    length = chunk * net.n_s
    depth = wq_own.shape[1]
    columns = wq_own.shape[2]
    heads = columns // HEAD
    pair = 2 * chunk
    buffers, rest = rest[:4], rest[4:]
    folds = []
    for _ in range(3):
        folds.append(Fold(net, tiles, total, *buffers, *rest[:4]))
        rest = rest[4:]
    att_fold, normed_fold, top_fold = folds
    line_sems = [rest[at : at + 3] for at in (0, 3, 6, 9)]
    rest = rest[12:]
    spread_sems, rest = rest[:5], rest[5:]
    gate_sum, up_sum, down_sum = [GridSum(net, *rest[at : at + 3]) for at in (0, 3, 6)]
    sums = (down_sum, gate_sum, up_sum)
    pk_sems, copy_sems, n1_sems, free_sem = rest[9:]
    copies = Copies(copy_sems)
    n1 = att_fold.mate_out

    packet[...] = jnp.zeros(packet.shape, F32)
    own = gain_one.shape[1]
    for at, part in enumerate((gain_one, shift_one, gain_two, shift_two)):
        packet[at : at + 1, 0:own] = part[...].astype(F32)
    packet[4:7, 0:own] = bias[...].astype(F32)
    def wq_part(f, half):
        if half is None:
            return wq.at[:, aligned(f * depth, depth), :]
        return wq.at[:, aligned(f * depth + half * (depth // 2), depth // 2), :]

    spread_q = Spread(net, wq_own, wq_part, spread_sems[0])
    spread_o, spread_g, spread_u, spread_d = [
        Spread(net, own, columns_of(full, depth), sems)
        for own, full, sems in zip((wo_own, wg_own, wu_own, wd_own), (wo, wg, wu, wd), spread_sems[1:])
    ]
    pk = Packets(net, packet, packets, pk_sems)
    line = Line(net, tok, rows_of(rows, chunk), *line_sems[0])
    gout_line = Line(net, gout_own, rows_of(gout, chunk), *line_sems[1])
    n2_line = Line(net, low, rows_of(rows, chunk), *line_sems[2])
    dm_line = Line(net, low, rows_of(rows, chunk), *line_sems[3])

    for ready in (line, spread_q, spread_o, spread_g, spread_u, spread_d, gout_line):
        ready.prepare()
    net.barrier()

    def pairs(which, hop):
        net.sides(hop, lambda other, side: which.pair(other))

    def blocks(hop, act):
        def once(other, side):
            @pl.when((hop > 0) | (side == 0))
            def _():
                act(other, side)

        net.sides(hop, once)

    pk.start()
    line.start()
    spread_q.start()
    pk.middle()
    pk.finish()
    pk.unpack(gains_o, width // (net.n_f * net.n_s))

    def project_block(other, side):
        span = aligned(other * pair, pair)
        gain, shift = gains_o[0:1, :], gains_o[1:2, :]

        for part in range(2):

            @pl.loop(0, chunk // 32)
            def _(i):
                at = aligned((2 * other + part) * chunk + i * 32, 32)
                scaled, _ = normalize(rows[at, :].astype(F32))
                n1[part, aligned(i * 32, 32), :] = (scaled * gain + shift).astype(BF)

        keeps = [
            pltpu.make_async_copy(
                n1.at[part], n1_o.at[aligned((2 * other + part) * chunk, chunk)], n1_sems.at[part]
            )
            for part in range(2)
        ]
        for copy in keeps:
            copy.start()
        left = n1[0:2].reshape(pair, width)
        cols = aligned(net.s * columns, columns)
        tables = cosine[span, :], sine[span, :]
        for kind in range(3):
            value = dot(left, wq[kind]) + gains_o[4 + kind : 5 + kind, cols]
            if kind == 0:
                q[span, :] = rotary(value, *tables).astype(BF)
            elif kind == 1:
                value = rotary(value, *tables)
                k[span, :] = value.astype(BF)
                kt[...] = value.T.astype(BF)
            else:
                v[...] = value.astype(BF)
                vt[:, span] = value.T.astype(BF)
        for copy in (
            pltpu.make_async_copy(kt, kt_o.at[:, span], n1_sems.at[2]),
            pltpu.make_async_copy(v, v_o.at[span], n1_sems.at[3]),
        ):
            copy.start()
            keeps.append(copy)
        for copy in keeps:
            copy.wait()

    line.here()
    for hop in range(1, net.n_l - 1):
        line.step(hop)
        if hop == 1:
            spread_q.relay()
        pairs(line, hop)
    spread_o.start()
    spread_q.finish()
    spread_g.start()
    pl.loop(0, net.n_l - 1)(lambda hop: blocks(hop, project_block))
    spread_o.relay()
    spread_u.start()
    line.step(net.n_l - 1)
    gout_line.start()
    pairs(line, net.n_l - 1)
    blocks(net.n_l - 1, project_block)
    spread_d.start()
    q_copy = copies.start(q, q_o)
    for pair_of in ((wq, wq_o), (k, k_o)):
        copies.start(*pair_of)
    spread_o.finish()
    line.finish()

    def attend(i):
        lo, hi = i * pair, (i + 1) * pair

        @pl.loop(0, heads)
        def _(head):
            lane = lax.broadcasted_iota(jnp.int32, (1, columns), 1)
            here = jnp.where(lane // HEAD == head, HEAD**-0.5, 0.0).astype(BF)
            visible = lax.broadcasted_iota(jnp.int32, (pair, pair), 0) <= lax.broadcasted_iota(
                jnp.int32, (pair, pair), 1
            )
            head_rows = aligned(head * HEAD, HEAD)
            query = q[lo:hi, :] * here
            near = jnp.where(visible, dot_nt(k[lo:hi, :], query), NEG_LARGE)
            highest = jnp.max(near, 0, keepdims=True)
            if i:
                far = dot_nt(k[0:lo, :], query)
                highest = jnp.maximum(highest, jnp.max(far, 0, keepdims=True))
            near = jnp.exp(near - highest)
            sum_of = jnp.sum(near, 0, keepdims=True)
            out = dot(vt[head_rows, lo:hi], near.astype(BF))
            if i:
                far = jnp.exp(far - highest)
                sum_of = sum_of + jnp.sum(far, 0, keepdims=True)
                out = out + dot(vt[head_rows, 0:lo], far.astype(BF))
            ot[head_rows, :] = out / sum_of
            lse_o[pl.ds(head, 1), lo:hi] = highest + jnp.log(sum_of)

        att[lo:hi, :] = ot[...].T.astype(BF)

    def produce_attended(place, write):
        for i in range(net.n_l):
            pl.when(place == i)(functools.partial(attend, i))
        left = att[aligned(place * pair, pair), :]

        @pl.loop(0, width // TILE)
        def _(j):
            cols = aligned(j * TILE, TILE)
            write(cols, dot(left, wo[:, cols]))

    def relays():
        gout_line.step(1)
        spread_g.relay()

    att_fold.begin(produce_attended, relays)
    copies.start(att, att_o)
    copies.start(wo, wo_o)
    att_fold.open_total()
    for at in range(1, net.n_l):
        att_fold.wave(at)
        if at + 1 < net.n_l:
            gout_line.step(at + 1)
        if at == 1:
            spread_u.relay()
        if at == min(2, net.n_l - 1):
            spread_d.relay()
    gain_two, shift_two = gains_o[2:3, :], gains_o[3:4, :]

    @pl.loop(0, chunk // 32)
    def _(i):
        span = aligned(i * 32, 32)
        value = rows[aligned(net.s * chunk + i * 32, 32), :].astype(F32) + total[span, :]
        mid[span, :] = value
        scaled, _ = normalize(value)
        low[span, :] = (scaled * gain_two + shift_two).astype(BF)

    n2_line.prepare()
    n2_line.start()
    att_fold.finish()
    gout_line.here()
    pl.loop(1, net.n_l)(lambda hop: pairs(gout_line, hop))

    def forward_block(other):
        span = aligned(other * pair, pair)
        right = rows[span, :]
        half = hidden.shape[0] // 2

        @pl.loop(0, 2)
        def _(part):
            units = aligned(part * half, half, 16)
            gate = dot_nt(wg[units, :], right)
            up = dot_nt(wu[units, :], right)
            back = dot_nt(wd[units, :], gout[span, :])
            sigma = jax.nn.sigmoid(gate)
            active = gate * sigma
            hidden[units, span] = (active * up).astype(BF)
            dgate[units, span] = (back * up * (sigma * (1.0 + gate * (1.0 - sigma)))).astype(BF)
            dup[units, span] = (back * active).astype(BF)

    def produce_normed(place, write):
        span = aligned(place * pair, pair)
        left, right = dgate[:, span].T, dup[:, span].T

        @pl.loop(0, width // TILE)
        def _(j):
            cols = aligned(j * TILE, TILE)
            write(cols, dot(left, wg[:, cols]) + dot(right, wu[:, cols]))

    def begin_normed(other, side, hop):
        @pl.when(hop > 1)
        def _():
            normed_fold.mate_sent(side)

        normed_fold.begin_one(other, side + (2 - side) * (1 // (hop + 1)), produce_normed)

    def forward_blocks(hop):
        def act(other, side):
            forward_block(other)

            @pl.when(jnp.logical_not(normed_fold.fed(side)))
            def _():
                begin_normed(other, side, hop)
                normed_fold.leave(other, side, hop)

        net.sides(hop, act)

    def begin_fed(hop):
        def act(other, side):
            @pl.when((hop == 0) | normed_fold.fed(side))
            def _():
                begin_normed(other, side, hop)

        blocks(hop, act)

    n2_line.here()
    for spread in (spread_g, spread_u, spread_d):
        spread.finish()
    forward_block(net.z)

    @pl.loop(1, net.n_l)
    def _(hop):
        n2_line.step(hop)
        pairs(n2_line, hop)
        forward_blocks(hop)
        begin_fed(hop - 1)

    begin_fed(net.n_l - 1)
    normed_fold.open_total()

    def weight_terms(task):
        at, kind = net.n_f - 1 - task // 3, task % 3
        cols = aligned(gate_sum.owner(at) * depth, depth)
        for way, (grid_sum, left, right) in enumerate(
            ((down_sum, hidden, gout), (gate_sum, dgate, rows), (up_sum, dup, rows))
        ):

            @pl.when(kind == way)
            def _():
                half = left.shape[0] // 2

                @pl.loop(0, 2)
                def _(part):
                    units = aligned(part * half, half, 16)
                    grid_sum.stage[at, units, :] = dot(left[units, :], right[:, cols]).astype(BF)

                grid_sum.first(at)

    tasks = 3 * net.n_f
    slots = 2 * normed_fold.pieces * (net.n_l - 1)
    each = -(-tasks // slots)

    def between(slot):
        @pl.loop(0, each)
        def _(i):
            pl.when(slot * each + i < tasks)(lambda: weight_terms(slot * each + i))

    for at in range(1, net.n_l):
        normed_fold.wave(at, near=True, between=between)
    n2_line.finish()

    def beside(act):
        act(net.mate)
        for side in range(2):
            pl.when(n2_line.goes_on(side))(lambda: act(net.s + 2 - 4 * side))

    beside(lambda to: pl.semaphore_signal(free_sem, 1, device_id={"seq": to}, device_id_type=MESH))

    def write_middle(i, span, value):
        value = value + gout[aligned(net.s * chunk + i * 32, 32), :].astype(F32)
        dmid_o[span, :] = value
        low[span, :] = value.astype(BF)

    terms_o[...] = jnp.zeros(terms_o.shape, F32)
    norm_backward(chunk, mid, total, gain_two, terms_o, 2, write_middle)
    ends = (net.z + net.n_l - 1) // net.n_l + (2 * net.n_l - 2 - net.z) // net.n_l
    pl.semaphore_wait(free_sem, 1 + ends)
    dm_line.prepare()
    dm_line.start()
    normed_fold.finish()

    def produce_top(place, write):
        left = hidden[:, aligned(place * pair, pair)].T

        @pl.loop(0, width // TILE)
        def _(j):
            cols = aligned(j * TILE, TILE)
            write(cols, dot(left, wd[:, cols]))

    copies.wait(q_copy)
    datt = q

    def back_block(other, side):
        span = aligned(other * pair, pair)
        datt[span, :] = dot_nt(rows[span, :], wo[...]).astype(BF)

    dm_line.here()
    dm_line.step(1)
    top_fold.begin(produce_top)
    back_block(net.z, 0)
    top_fold.open_total()
    for at in range(1, net.n_l):
        if at + 1 < net.n_l:
            dm_line.step(at + 1)
        top_fold.wave(at)
        pairs(dm_line, at)
        net.sides(at, back_block)
    copies.start(datt, datt_o)
    copies.start(rows, dm_o)

    @pl.loop(0, chunk // 32)
    def _(i):
        span = aligned(i * 32, 32)
        top_fold.out[net.z, span, :] = (mid[span, :] + total[span, :]).astype(BF)

    copies.start(top_fold.out.at[net.z], top_o)
    top_fold.finish()
    gout_line.finish()
    dm_line.finish()
    hands = []
    for grid_sum, out in zip(sums, (down_o, gate_o, up_o)):
        grid_sum.sum_first()
        hands.extend(grid_sum.hand_on(out))
        for copy in grid_sum.hand_on(out):
            copy.start()
    for grid_sum in sums:
        grid_sum.finish_first()
    for copy in hands:
        copy.wait()
    copies.wait()


def layer_part(tokens, norms, wq, wo, wg, wu, wd, gout, tables):
    chunk, width = tokens.shape
    n_f, n_s = lax.axis_size("fsdp"), lax.axis_size("seq")
    length = chunk * n_s
    depth, columns = wq.shape[1:]
    units = wg.shape[0]
    shape = jax.ShapeDtypeStruct
    wide, head, turned, weight = (length, width), (length, columns), (units, length), (units, width)
    return pl.pallas_call(
        layer_kernel,
        name="layer",
        out_shape=[
            shape(head, BF),
            shape(head, BF),
            shape((columns, length), BF),
            shape(head, BF),
            shape(head, BF),
            shape((8, length), F32),
            shape(wide, BF),
            shape((SMALL, width), F32),
            shape((3, width, columns), BF),
            shape((columns, width), BF),
            shape(wide, BF),
            shape(head, BF),
            shape((chunk, width), F32),
            shape((chunk, width), BF),
            shape((SMALL, width), F32),
            *[shape((GridEnd.count(n_f), units // 2, depth), BF)] * 3,
        ],
        in_specs=[ANY, *[VMEM] * 5, *[ANY] * 6, VMEM, VMEM],
        out_specs=[*[ANY] * 5, VMEM, ANY, VMEM, *[ANY] * 4, VMEM, ANY, VMEM, *[ANY] * 3],
        scratch_shapes=[
            pltpu.VMEM(wide, BF),
            pltpu.VMEM(wide, BF),
            pltpu.VMEM((3, width, columns), BF),
            pltpu.VMEM((columns, width), BF),
            *[pltpu.VMEM(weight, BF)] * 3,
            pltpu.VMEM(head, BF),
            pltpu.VMEM(head, BF),
            pltpu.VMEM((columns, 2 * chunk), BF),
            pltpu.VMEM((2 * chunk, columns), BF),
            pltpu.VMEM((columns, length), BF),
            pltpu.VMEM((columns, 2 * chunk), F32),
            pltpu.VMEM(head, BF),
            *[pltpu.VMEM(turned, BF)] * 3,
            pltpu.VMEM((chunk, width), F32),
            pltpu.VMEM((chunk, width), BF),
            pltpu.VMEM((SMALL, 128), F32),
            pltpu.VMEM((n_s, n_f, SMALL, 128), F32),
            *Fold.shared(chunk, width),
            *Fold.buffers(n_s, chunk, width),
            *Fold.sems(n_s) * 3,
            *Line.sems(n_s) * 4,
            *[pltpu.SemaphoreType.DMA((Spread.count(n_f),))] * 5,
            *GridSum.scratch(n_f, units, depth) * 3,
            pltpu.SemaphoreType.DMA((Packets.count(n_f, n_s),)),
            pltpu.SemaphoreType.DMA((8,)),
            pltpu.SemaphoreType.DMA((4,)),
            pltpu.SemaphoreType.REGULAR,
        ],
        compiler_params=pltpu.CompilerParams(
            collective_id=1, has_side_effects=True, vmem_limit_bytes=VMEM_BYTES
        ),
        cost_estimate=pl.CostEstimate(
            flops=2 * length * width * (4 * columns + 9 * units),
            bytes_accessed=8 * length * width,
            transcendentals=length * (length * columns // HEAD + units),
        ),
    )(tokens, *norms, wq, wo, wg, wu, wd, gout, *tables)


def back_kernel(
    datt_in,
    q_in,
    k_in,
    kt_in,
    v_in,
    att_in,
    wq_in,
    n1_in,
    dm_in,
    down_in,
    gate_in,
    up_in,
    lse,
    tok,
    dmid,
    gains,
    terms_in,
    cosine,
    sine,
    gin_o,
    small_o,
    out_o,
    qkv_o,
    down_o,
    gate_o,
    up_o,
    datt,
    q,
    k,
    kt,
    v,
    att,
    wq,
    n1,
    dm,
    query,
    upstream,
    inners,
    dk,
    dv,
    dqt,
    dproj,
    terms,
    tiles,
    total,
    *rest,
):
    net = Net()
    chunk, width = tok.shape
    length, columns = q_in.shape
    heads = columns // HEAD
    pair = 2 * chunk
    depth = width // net.n_f
    block = 256
    buffers, rest = rest[:4], rest[4:]
    fold_sems, rest = rest[:4], rest[4:]
    packet_scratch, rest = rest[:5], rest[5:]
    out_sum, qkv_sum = GridSum(net, *rest[:3]), GridSum(net, *rest[3:6])
    ends = [GridEnd(net, *rest[at : at + 3]) for at in (6, 9, 12)]
    copy_sems, column_sems = rest[15:]

    copies = Copies(copy_sems)
    loads = [
        copies.start(src, dst)
        for src, dst in (
            (datt_in, datt),
            (q_in, q),
            (k_in, k),
            (kt_in, kt),
            (v_in, v),
            (att_in, att),
            (wq_in, wq),
            (down_in, ends[0].sums),
            (gate_in, ends[1].sums),
            (up_in, ends[2].sums),
        )
    ]
    def load(at, way):
        src, dst = ((n1_in, n1), (dm_in, dm))[way]
        cols = aligned(qkv_sum.owner(at) * depth, depth)
        return pltpu.make_async_copy(src.at[:, cols], dst.at[at % 2], column_sems.at[way, at % 2])

    for at in range(net.n_f - 1, max(net.n_f - 3, -1), -1):
        for way in range(2):
            load(at, way).start()

    @pl.loop(0, length // block)
    def _(i):
        span = aligned(i * block, block)
        dk[span, :] = jnp.zeros((block, columns), F32)
        dv[span, :] = jnp.zeros((block, columns), F32)

    net.barrier()
    copies.wait(*loads[7:])
    for end in ends:
        end.start()
    copies.wait(*loads[:6])

    of_head = (
        lax.broadcasted_iota(jnp.int32, (8, columns), 1) // HEAD
        == lax.broadcasted_iota(jnp.int32, (8, columns), 0)
    ).astype(F32)

    @pl.loop(0, length // block)
    def _(i):
        span = aligned(i * block, block)
        product = datt[span, :].astype(F32) * att[span, :].astype(F32)
        inners[:, span] = lax.dot_general(
            of_head,
            product,
            (((1,), (1,)), ((), ())),
            precision=lax.Precision.HIGHEST,
            preferred_element_type=F32,
        )

    @pl.loop(0, heads)
    def _(head):
        lane = lax.broadcasted_iota(jnp.int32, (1, columns), 1)
        here = jnp.where(lane // HEAD == head, 1.0, 0.0).astype(BF)
        scale = HEAD**-0.5
        visible = lax.broadcasted_iota(jnp.int32, (block, block), 0) <= lax.broadcasted_iota(
            jnp.int32, (block, block), 1
        )
        head_rows = aligned(head * HEAD, HEAD)

        @pl.loop(0, length // block)
        def _(i):
            span = aligned(i * block, block)
            query[span, :] = q[span, :] * (here * scale)
            upstream[span, :] = datt[span, :] * here

        for j in range(length // block):
            at, end = j * block, (j + 1) * block
            keys, values, turned = k[at:end, :], v[at:end, :], kt[head_rows, at:end]

            def part(lo, hi, near):
                probs = jnp.exp(dot_nt(keys, query[lo:hi, :]) - lse[pl.ds(head, 1), lo:hi])
                if near:
                    probs = jnp.where(visible, probs, 0.0)
                grads = dot_nt(values, upstream[lo:hi, :])
                scores = (probs * (grads - inners[pl.ds(head, 1), lo:hi])).astype(BF)
                out = dot(turned, scores)
                dqt[head_rows, lo:hi] = dqt[head_rows, lo:hi] + out if j else out
                return dot(probs.astype(BF), upstream[lo:hi, :]), dot(scores, query[lo:hi, :])

            value_grads, key_grads = part(at, end, True)
            if end < length:
                more_values, more_keys = part(end, length, False)
                value_grads, key_grads = value_grads + more_values, key_grads + more_keys
            dv[at:end, :] = dv[at:end, :] + value_grads
            dk[at:end, :] = dk[at:end, :] + key_grads

    terms[...] = terms_in[...]
    bias_cols = aligned(net.s * columns, columns)

    @pl.loop(0, length // block)
    def _(i):
        span = aligned(i * block, block)
        tables = cosine[span, :], -sine[span, :]
        parts = [
            rotary((dqt[:, span].T * HEAD**-0.5).astype(BF).astype(F32), *tables).astype(BF),
            rotary(dk[span, :].astype(BF).astype(F32), *tables).astype(BF),
            dv[span, :].astype(BF),
        ]
        for kind in range(3):
            dproj[kind, span, :] = parts[kind]
            row = slice(4 + kind, 5 + kind)
            terms[row, bias_cols] = terms[row, bias_cols] + jnp.sum(parts[kind].astype(F32), 0, keepdims=True)

    def weight_terms(task):
        at = net.n_f - 1 - task // 2

        def loaded(way):
            load(at, way).wait()

        def next_load(way):
            pl.when(at >= 2)(lambda: load(at - 2, way).start())

        @pl.when(task % 2 == 0)
        def _():
            loaded(0)
            left = n1[at % 2].T
            for kind in range(3):
                qkv_sum.stage[at, kind * depth : (kind + 1) * depth, :] = dot(left, dproj[kind]).astype(BF)
            next_load(0)
            qkv_sum.first(at)

        @pl.when(task % 2 == 1)
        def _():
            loaded(1)
            out_sum.stage[at] = dot_tn(att[...], dm[at % 2]).astype(BF)
            next_load(1)
            out_sum.first(at)

    def produce(place, write):
        span = aligned(place * pair, pair)

        @pl.loop(0, width // TILE)
        def _(j):
            cols = aligned(j * TILE, TILE)
            value = dot_nt(dproj[0, span, :], wq[0, cols, :])
            for kind in range(1, 3):
                value = value + dot_nt(dproj[kind, span, :], wq[kind, cols, :])
            write(cols, value)

    fold = Fold(net, tiles, total, *buffers, *fold_sems)
    copies.wait()
    fold.begin(produce)
    fold.open_total()
    tasks = 2 * net.n_f
    waves = max(net.n_l - 2, 1)
    each = -(-tasks // (2 * fold.pieces * waves))

    def between(slot):
        @pl.loop(0, each)
        def _(i):
            pl.when(slot * each + i < tasks)(lambda: weight_terms(slot * each + i))

    for at in range(1, waves + 1):
        fold.wave(at, between=between)
    for at in range(waves + 1, net.n_l):
        fold.wave(at)

    def write_input(i, span, value):
        gin_o[span, :] = value + dmid[span, :]

    norm_backward(chunk, tok, total, gains[0:1, :], terms, 0, write_input)
    packet_sum = PacketSum(net, *packet_scratch)
    packet_sum.start(terms, width // (net.n_f * net.n_s))
    for grid_sum in (qkv_sum, out_sum):
        grid_sum.second()
    packet_sum.middle()
    for end, out in zip(ends, (down_o, gate_o, up_o)):
        end.last(out)
    packet_sum.finish(small_o)
    fold.finish()
    for grid_sum, out in ((qkv_sum, qkv_o), (out_sum, out_o)):
        grid_sum.last(out)
        grid_sum.finish()


def back_part(datt, q, k, kt, v, att, wq, n1, dm, down, gate, up, lse, tokens, dmid, gains, terms, tables):
    chunk, width = tokens.shape
    n_f, n_s = lax.axis_size("fsdp"), lax.axis_size("seq")
    length, columns = q.shape
    depth = width // n_f
    units = 2 * gate.shape[1]
    shape = jax.ShapeDtypeStruct
    return pl.pallas_call(
        back_kernel,
        name="back",
        out_shape=[
            shape((chunk, width), F32),
            shape((SMALL, 128), F32),
            shape((columns, depth), F32),
            shape((3 * depth, columns), F32),
            *[shape((units, depth), F32)] * 3,
        ],
        in_specs=[ANY] * 12 + [VMEM] * 7,
        out_specs=[VMEM] * 7,
        scratch_shapes=[
            pltpu.VMEM((length, columns), BF),
            pltpu.VMEM((length, columns), BF),
            pltpu.VMEM((length, columns), BF),
            pltpu.VMEM((columns, length), BF),
            pltpu.VMEM((length, columns), BF),
            pltpu.VMEM((length, columns), BF),
            pltpu.VMEM((3, width, columns), BF),
            pltpu.VMEM((2, length, depth), BF),
            pltpu.VMEM((2, length, depth), BF),
            pltpu.VMEM((length, columns), BF),
            pltpu.VMEM((length, columns), BF),
            pltpu.VMEM((8, length), F32),
            pltpu.VMEM((length, columns), F32),
            pltpu.VMEM((length, columns), F32),
            pltpu.VMEM((columns, length), F32),
            pltpu.VMEM((3, length, columns), BF),
            pltpu.VMEM((SMALL, width), F32),
            *Fold.shared(chunk, width),
            *Fold.buffers(n_s, chunk, width),
            *Fold.sems(n_s),
            *PacketSum.scratch(n_f, n_s),
            *GridSum.scratch(n_f, columns, depth),
            *GridSum.scratch(n_f, 3 * depth, columns),
            *GridEnd.scratch(n_f, units, depth) * 3,
            pltpu.SemaphoreType.DMA((10,)),
            pltpu.SemaphoreType.DMA((2, 2)),
        ],
        compiler_params=pltpu.CompilerParams(
            collective_id=3, has_side_effects=True, vmem_limit_bytes=VMEM_BYTES
        ),
        cost_estimate=pl.CostEstimate(
            flops=2 * length * columns * (8 * width + 5 * length),
            bytes_accessed=4 * length * width,
            transcendentals=length * length * columns // HEAD,
        ),
    )(datt, q, k, kt, v, att, wq, n1, dm, down, gate, up, lse, tokens, dmid, gains, terms, *tables)


def outputs_kernel(small, *refs):
    sources, targets, parts = refs[:7], refs[7:14], refs[14:]
    own = parts[0].shape[1]
    for src, dst in zip(sources, targets):
        dst[...] = src[...]
    for at in range(4):
        parts[at][...] = small[at : at + 1, 0:own]
    parts[4][...] = small[4:7, 0:own]


def outputs_part(small, own, *arrays):
    shape = jax.ShapeDtypeStruct
    return pl.pallas_call(
        outputs_kernel,
        name="outputs",
        out_shape=[shape(v.shape, v.dtype) for v in arrays]
        + [shape((1, own), F32)] * 4
        + [shape((3, own), F32)],
        in_specs=[VMEM] * 8,
        out_specs=[VMEM] * 12,
        compiler_params=pltpu.CompilerParams(vmem_limit_bytes=VMEM_BYTES),
    )(small, *arrays)


def per_device(
    tokens,
    gain_one,
    shift_one,
    w_qkv,
    b_qkv,
    w_out,
    gain_two,
    shift_two,
    w_gate,
    w_up,
    w_down,
    grad_output,
):
    length = tokens.shape[1] * lax.axis_size("seq")
    width = gain_one.shape[0]
    norms = [v[None] for v in (gain_one, shift_one, gain_two, shift_two)] + [b_qkv]
    tables = rotary_tables(length)
    q, k, kt, v, att, lse, n1, gains, wq, _, dm, datt, dmid, top, terms, gate, up, down = layer_part(
        tokens[0], norms, w_qkv.transpose(1, 0, 2), w_out, w_gate.T, w_up.T, w_down, grad_output[0], tables
    )
    grad_input, small, out, qkv, down, gate, up = back_part(
        datt, q, k, kt, v, att, wq, n1, dm, down, gate, up, lse, tokens[0], dmid, gains, terms, tables
    )

    top, grad_input, qkv, out, gate, up, down, one, shift, two, shift_to, bias = outputs_part(
        small, width, top, grad_input, qkv, out, gate, up, down
    )
    return (
        top[None],
        grad_input[None],
        one[0],
        shift[0],
        qkv.reshape(3, -1, qkv.shape[1]).transpose(1, 0, 2),
        bias,
        out,
        two[0],
        shift_to[0],
        gate.T,
        up.T,
        down,
    )


def solution(mesh):
    whole = P(("fsdp", "seq"))
    rows = P("fsdp", "seq", None)
    inner = P("seq", "fsdp")
    outer = P("fsdp", "seq")
    heads = P("fsdp", None, "seq")
    bias = P(None, ("fsdp", "seq"))
    return jax.shard_map(
        per_device,
        mesh=mesh,
        in_specs=(rows, whole, whole, heads, bias, inner, whole, whole, outer, outer, inner, rows),
        out_specs=(rows, rows, whole, whole, heads, bias, inner, whole, whole, outer, outer, inner),
        check_vma=False,
    )
```

profile of v0, /device:TPU:8, one launch (start us, length us, event | category | flops | bytes accessed | tf_op | source)
XLA Modules:
  0.0 332.8 jit_solution(2417452467861470254)
XLA Ops:
  0.6 247.0 %layer.1 = (bf16[1024,256]{1,0:T(8,128)(2,1)}, bf16[1024,256]{1,0:T(8,128)(2,1)}, bf16[256,1024]{1,0:T(8,128)(2,1)}, bf16[1024,256]{1,0:T(8,128)(2,1)}, bf16[102...) custom-call(bf16[128,2048]{1,0:T(8,128)(2,1)} %bitcast.28, ...), custom_call_target="tpu_custom_call" | custom-call | flops 30870077440 | bytes 16777216 | tf_op jit(solution)/shard_map/layer/pallas_call | solution.py:1279
  247.7 78.3 %back.1 = (f32[128,2048]{1,0:T(8,128)}, f32[8,128]{1,0:T(8,128)}, f32[256,512]{1,0:T(8,128)}, f32[1536,256]{1,0:T(8,128)}, f32[704,512]{1,0:T(8,128)}, /*index=5*/f32[704,512]{1,0:T(8,128)}, f32[704,512]{1,0:T(8,128)}) custom-call(bf16[1024,256]{1,0:T(8,128)(2,1)} %get-tuple-element.48.datt_in, bf16[1024,256]{1,0:T(8,128)(2,1)} %get-tuple-element.49.q_in, ...), custom_call_target="tpu_custom_call" | custom-call | flops 11274289152 | bytes 8388608 | tf_op jit(solution)/shard_map/back/pallas_call | solution.py:1591
  326.0 6.6 %outputs.1 = (bf16[128,2048]{1,0:T(8,128)(2,1)}, f32[128,2048]{1,0:T(8,128)}, f32[1536,256]{1,0:T(8,128)}, f32[256,512]{1,0:T(8,128)}, f32[704,512]{1,0:T(8,128)...) custom-call(f32[8,128]{1,0:T(8,128)} %get-tuple-element.64.small, ...), custom_call_target="tpu_custom_call" | custom-call | tf_op jit(solution)/shard_map/outputs/pallas_call | solution.py:1654
where the time goes:
time: 333 us
  Pallas kernels  332 us (100%)
    pallas_call x1, Pallas kernels, layer_part(): pl.pallas_call(layer_kernel, name='layer', out_shape=[shape(head, BF), sh...  247 us
    pallas_call x1, Pallas kernels, back_part(): pl.pallas_call(back_kernel, name='back', out_shape=[shape((chunk, width),...  78.3 us

commit v1 on v0

--- a/solution.py
+++ b/solution.py
@@ -433,7 +433,7 @@
         ]
 
     @staticmethod
-    def sems(n_s, pieces=4):
+    def sems(n_s, pieces=2):
         n_l = n_s // 2
         return [
             pltpu.SemaphoreType.DMA((3, pieces)),

time: 333 us -> 339 us (1.018); the launches traced: 333 us -> 333 us
  no operation moved by 1% of the time
where the time goes in v1:
time: 339 us; the launch traced here: 333 us
  Pallas kernels  332 us (98%)
    pallas_call x1, Pallas kernels, layer_part(): pl.pallas_call(layer_kernel, name='layer', out_shape=[shape(head, BF), sh...  248 us
    pallas_call x1, Pallas kernels, back_part(): pl.pallas_call(back_kernel, name='back', out_shape=[shape((chunk, width),...  77.9 us

profile of v1, /device:TPU:8, one launch (start us, length us, event | category | flops | bytes accessed | tf_op | source)
XLA Modules:
  0.0 332.9 jit_solution(5822659268669243851)
XLA Ops:
  0.6 247.6 %layer.1 = (bf16[1024,256]{1,0:T(8,128)(2,1)}, bf16[1024,256]{1,0:T(8,128)(2,1)}, bf16[256,1024]{1,0:T(8,128)(2,1)}, bf16[1024,256]{1,0:T(8,128)(2,1)}, bf16[102...) custom-call(bf16[128,2048]{1,0:T(8,128)(2,1)} %bitcast.28, ...), custom_call_target="tpu_custom_call" | custom-call | flops 30870077440 | bytes 16777216 | tf_op jit(solution)/shard_map/layer/pallas_call | solution.py:1279
  248.2 77.9 %back.1 = (f32[128,2048]{1,0:T(8,128)}, f32[8,128]{1,0:T(8,128)}, f32[256,512]{1,0:T(8,128)}, f32[1536,256]{1,0:T(8,128)}, f32[704,512]{1,0:T(8,128)}, /*index=5*/f32[704,512]{1,0:T(8,128)}, f32[704,512]{1,0:T(8,128)}) custom-call(bf16[1024,256]{1,0:T(8,128)(2,1)} %get-tuple-element.48.datt_in, bf16[1024,256]{1,0:T(8,128)(2,1)} %get-tuple-element.49.q_in, ...), custom_call_target="tpu_custom_call" | custom-call | flops 11274289152 | bytes 8388608 | tf_op jit(solution)/shard_map/back/pallas_call | solution.py:1591
  326.1 6.6 %outputs.1 = (bf16[128,2048]{1,0:T(8,128)(2,1)}, f32[128,2048]{1,0:T(8,128)}, f32[1536,256]{1,0:T(8,128)}, f32[256,512]{1,0:T(8,128)}, f32[704,512]{1,0:T(8,128)...) custom-call(f32[8,128]{1,0:T(8,128)} %get-tuple-element.64.small, ...), custom_call_target="tpu_custom_call" | custom-call | tf_op jit(solution)/shard_map/outputs/pallas_call | solution.py:1654

commit v2 on v0

--- a/solution.py
+++ b/solution.py
@@ -565,6 +565,47 @@
 
                 if between is not None:
                     between(((at - 1) * 2 + turn) * self.pieces + piece)
+
+    def passes_between(self, wave, near, between):
+        net = self.net
+        above = wave if near else net.n_l - wave
+
+        @pl.loop(0, 2)
+        def _(turn):
+            side = (1 - (2 * net.z) // net.n_l + turn) % 2
+            target = net.n_l - 1 - above + (2 * above - net.n_l + 1) * side
+            hop = (target - net.z) * (2 * side - 1)
+
+            @self.each_piece
+            def _(piece):
+                @pl.when((hop > 0) & self.fed(side))
+                def _():
+                    self.pass_piece(target, side, hop, piece, True)
+
+                between(turn, piece)
+
+    def finals(self):
+        net = self.net
+
+        @self.each_piece
+        def _(piece):
+            self.to_mate(net.z, 0, piece).wait_recv()
+            span = self.span(piece)
+            self.total[span, :] = self.out[net.z, span, :].astype(F32) + self.mate_in[net.z, span, :].astype(F32)
+
+        @pl.loop(0, 2)
+        def _(turn):
+            side = (1 - (2 * net.z) // net.n_l + turn) % 2
+
+            @pl.when(self.fed(side))
+            def _():
+                slot = net.z + (net.n_l - net.z) * (1 - side)
+
+                @self.each_piece
+                def _(piece):
+                    span = self.span(piece)
+                    self.came(slot, piece)
+                    self.total[span, :] = self.total[span, :] + self.coming[slot, span, :].astype(F32)
 
     def finish(self):
         net = self.net
@@ -1021,7 +1062,6 @@
     gout_line.start()
     pairs(line, net.n_l - 1)
     blocks(net.n_l - 1, project_block)
-    spread_d.start()
     q_copy = copies.start(q, q_o)
     for pair_of in ((wq, wq_o), (k, k_o)):
         copies.start(*pair_of)
@@ -1069,16 +1109,19 @@
 
     def relays():
         gout_line.step(1)
-        spread_g.relay()
+        spread_d.start()
 
     att_fold.begin(produce_attended, relays)
     copies.start(att, att_o)
     copies.start(wo, wo_o)
+    if net.n_l > 2:
+        gout_line.step(2)
     att_fold.open_total()
+    spread_g.relay()
     for at in range(1, net.n_l):
+        if 2 < at + 1 < net.n_l:
+            gout_line.step(at + 1)
         att_fold.wave(at)
-        if at + 1 < net.n_l:
-            gout_line.step(at + 1)
         if at == 1:
             spread_u.relay()
         if at == min(2, net.n_l - 1):
@@ -1145,11 +1188,9 @@
 
     def begin_fed(hop):
         def act(other, side):
-            @pl.when((hop == 0) | normed_fold.fed(side))
-            def _():
-                begin_normed(other, side, hop)
-
-        blocks(hop, act)
+            pl.when(normed_fold.fed(side))(lambda: begin_normed(other, side, hop))
+
+        net.sides(hop, act)
 
     n2_line.here()
     for spread in (spread_g, spread_u, spread_d):
@@ -1160,11 +1201,11 @@
     def _(hop):
         n2_line.step(hop)
         pairs(n2_line, hop)
+        pl.when(hop == 1)(lambda: normed_fold.begin_one(net.z, 2, produce_normed))
         forward_blocks(hop)
-        begin_fed(hop - 1)
+        pl.when(hop > 1)(lambda: begin_fed(hop - 1))
 
     begin_fed(net.n_l - 1)
-    normed_fold.open_total()
 
     def weight_terms(task):
         at, kind = net.n_f - 1 - task // 3, task % 3
@@ -1185,16 +1226,19 @@
                 grid_sum.first(at)
 
     tasks = 3 * net.n_f
-    slots = 2 * normed_fold.pieces * (net.n_l - 1)
-    each = -(-tasks // slots)
-
-    def between(slot):
-        @pl.loop(0, each)
-        def _(i):
-            pl.when(slot * each + i < tasks)(lambda: weight_terms(slot * each + i))
-
-    for at in range(1, net.n_l):
-        normed_fold.wave(at, near=True, between=between)
+    waves = max(net.n_l - 2, 1)
+    each = -(-tasks // (2 * normed_fold.pieces * waves))
+    for wave in range(net.n_l - waves, net.n_l):
+
+        def between(turn, piece):
+            slot = ((wave - net.n_l + waves) * 2 + turn) * normed_fold.pieces + piece
+
+            @pl.loop(0, each)
+            def _(i):
+                pl.when(slot * each + i < tasks)(lambda: weight_terms(slot * each + i))
+
+        normed_fold.passes_between(wave, True, between)
+    normed_fold.finals()
     n2_line.finish()
 
     def beside(act):
@@ -1433,10 +1477,14 @@
         dv[span, :] = jnp.zeros((block, columns), F32)
 
     net.barrier()
-    copies.wait(*loads[7:])
-    for end in ends:
-        end.start()
     copies.wait(*loads[:6])
+
+    def start_ends():
+        for load_of in loads[7:]:
+            load_of.wait()
+        for end in ends:
+            end.start()
+
 
     of_head = (
         lax.broadcasted_iota(jnp.int32, (8, columns), 1) // HEAD
@@ -1470,6 +1518,8 @@
             span = aligned(i * block, block)
             query[span, :] = q[span, :] * (here * scale)
             upstream[span, :] = datt[span, :] * here
+
+        pl.when(head == min(1, heads - 1))(start_ends)
 
         for j in range(length // block):
             at, end = j * block, (j + 1) * block
@@ -1546,7 +1596,7 @@
             write(cols, value)
 
     fold = Fold(net, tiles, total, *buffers, *fold_sems)
-    copies.wait()
+    copies.wait(loads[6])
     fold.begin(produce)
     fold.open_total()
     tasks = 2 * net.n_f
@@ -1620,7 +1670,7 @@
             pltpu.VMEM((SMALL, width), F32),
             *Fold.shared(chunk, width),
             *Fold.buffers(n_s, chunk, width),
-            *Fold.sems(n_s),
+            *Fold.sems(n_s, 8),
             *PacketSum.scratch(n_f, n_s),
             *GridSum.scratch(n_f, columns, depth),
             *GridSum.scratch(n_f, 3 * depth, columns),

time: 333 us -> 330 us (level)
  no operation moved by 1% of the time
where the time goes in v2:
time: 330 us
  Pallas kernels  329 us (100%)
    pallas_call x1, Pallas kernels, layer_part(): pl.pallas_call(layer_kernel, name='layer', out_shape=[shape(head, BF), sh...  244 us
    pallas_call x1, Pallas kernels, back_part(): pl.pallas_call(back_kernel, name='back', out_shape=[shape((chunk, width),...  79.1 us
    pallas_call x1, Pallas kernels, outputs_part(): pl.pallas_call(outputs_kernel, name='outputs', out_shape=[shape(v.shape,...  6.64 us

profile of v2, /device:TPU:8, one launch (start us, length us, event | category | flops | bytes accessed | tf_op | source)
XLA Modules:
  0.0 330.3 jit_solution(1296574387429314862)
XLA Ops:
  0.6 243.7 %layer.1 = (bf16[1024,256]{1,0:T(8,128)(2,1)}, bf16[1024,256]{1,0:T(8,128)(2,1)}, bf16[256,1024]{1,0:T(8,128)(2,1)}, bf16[1024,256]{1,0:T(8,128)(2,1)}, bf16[102...) custom-call(bf16[128,2048]{1,0:T(8,128)(2,1)} %bitcast.28, ...), custom_call_target="tpu_custom_call" | custom-call | flops 30870077440 | bytes 16777216 | tf_op jit(solution)/shard_map/layer/pallas_call | solution.py:1323
  244.4 79.1 %back.1 = (f32[128,2048]{1,0:T(8,128)}, f32[8,128]{1,0:T(8,128)}, f32[256,512]{1,0:T(8,128)}, f32[1536,256]{1,0:T(8,128)}, f32[704,512]{1,0:T(8,128)}, /*index=5*/f32[704,512]{1,0:T(8,128)}, f32[704,512]{1,0:T(8,128)}) custom-call(bf16[1024,256]{1,0:T(8,128)(2,1)} %get-tuple-element.48.datt_in, bf16[1024,256]{1,0:T(8,128)(2,1)} %get-tuple-element.49.q_in, ...), custom_call_target="tpu_custom_call" | custom-call | flops 11274289152 | bytes 8388608 | tf_op jit(solution)/shard_map/back/pallas_call | solution.py:1641
  323.5 6.6 %outputs.1 = (bf16[128,2048]{1,0:T(8,128)(2,1)}, f32[128,2048]{1,0:T(8,128)}, f32[1536,256]{1,0:T(8,128)}, f32[256,512]{1,0:T(8,128)}, f32[704,512]{1,0:T(8,128)...) custom-call(f32[8,128]{1,0:T(8,128)} %get-tuple-element.64.small, ...), custom_call_target="tpu_custom_call" | custom-call | tf_op jit(solution)/shard_map/outputs/pallas_call | solution.py:1704
